TPU v7x, 32 devices: a whole 2x2x4 slice. The times are simulated.
32 devices in a mesh: groups: 2 (over y), rows: 4 (over z), cols: 4 (over x, core).
Axes of the slice: x: 2, y: 2, z: 4, core: 2. Of those that a mesh axis runs over, the one named last changes fastest.
Arguments:
- inputs: bfloat16 [32, 6144], P(None, ('groups', 'rows', 'cols')), parts along dimension 1, may hold values from -6 to 6
- task_ids: int32 [6144], P(('groups', 'rows', 'cols')), parts along dimension 0, may hold values from 0 to 2999
- scale_table: float32 [3000], replicated, may hold values from 0.5 to 2
- probes: float32 [16, 6144], P(None, ('groups', 'rows', 'cols')), parts along dimension 1, may hold values from -6 to 6
- solves: float32 [16, 6144], P(None, ('groups', 'rows', 'cols')), parts along dimension 1, may hold values from -6 to 6
- alpha_solve: float32 [6144], P(('groups', 'rows', 'cols')), parts along dimension 0, may hold values from -6 to 6
- w_in: bfloat16 [32, 256], replicated, may hold values from -1 to 1
- b_in: float32 [256], replicated, may hold values from -3 to 3
- w_out: bfloat16 [256, 64], replicated, may hold values from -0.375 to 0.375
Outputs:
- feat_grad: float32 [64, 6144], P(None, ('groups', 'rows', 'cols')), parts along dimension 1
- grad_w_in: float32 [64, 256], P('groups'), parts along dimension 0
- grad_b_in: float32 [512], P('groups'), parts along dimension 0
- grad_w_out: float32 [512, 64], P('groups'), parts along dimension 0
There are 2 independent parts, one for each index of `groups`. A program takes and returns all parts, laid end to end along the dimension named above; an argument that names none is the same for every part. Nothing has to cross between parts.
All inputs are finite; a program needn't handle non-finite values.
Results may differ from a plain program's by a relative error of at most 0.0098.
Values may be sent and summed in bfloat16 or wider, within the bound.
A program may use at most 64 MiB of HBM per device.

v0:
```python
import math

import jax
import jax.numpy as jnp
from jax import lax
from jax.sharding import PartitionSpec as P

kernel_rate = 1.0


def project(inputs, w_in, b_in, w_out):
    preact = (
        lax.dot_general(w_in, inputs, (((0,), (0,)), ((), ())), preferred_element_type=jnp.float32)
        + b_in[:, None]
    )
    hidden = jax.nn.silu(preact).astype(jnp.bfloat16)
    feat_rows = lax.dot_general(
        w_out, hidden, (((0,), (0,)), ((), ())), preferred_element_type=jnp.float32
    ).astype(jnp.bfloat16)
    return (preact, hidden, feat_rows)


def tile_terms(row_feats, row_vecs, col_feats, col_vecs):
    probe_count = (row_vecs.shape[0] - 1) // 2
    feat_width = row_feats.shape[0]
    row_float = row_feats.astype(jnp.float32)
    col_float = col_feats.astype(jnp.float32)
    row_norm = jnp.sum(row_float * row_float, 0)
    col_norm = jnp.sum(col_float * col_float, 0)
    inner_prod = lax.dot_general(
        row_feats, col_feats, (((0,), (0,)), ((), ())), preferred_element_type=jnp.float32
    )
    kernel = jnp.exp(
        -(row_norm[:, None] + col_norm[None, :] - 2.0 * inner_prod) * (kernel_rate / feat_width)
    )
    swapped = jnp.concatenate([col_vecs[probe_count : 2 * probe_count], col_vecs[:probe_count]], 0)
    pair_term = lax.dot_general(
        row_vecs[: 2 * probe_count],
        swapped,
        (((0,), (0,)), ((), ())),
        preferred_element_type=jnp.float32,
    ) / (2.0 * probe_count)
    pair_term = (
        pair_term
        - row_vecs[2 * probe_count].astype(jnp.float32)[:, None]
        * col_vecs[2 * probe_count].astype(jnp.float32)[None, :]
    )
    weight = pair_term * kernel
    weight_sum = jnp.sum(weight, 1)
    totals = lax.dot_general(
        col_feats,
        weight.astype(jnp.bfloat16),
        (((1,), (1,)), ((), ())),
        preferred_element_type=jnp.float32,
    )
    return (totals, weight_sum)


def body(inputs, task_ids, scale_table, probes, solves, alpha_solve, w_in, b_in, w_out):
    trial_count = inputs.shape[1]
    feat_width = w_out.shape[1]
    preact, hidden, feat_rows = project(inputs, w_in, b_in, w_out)
    trial_scale = jnp.take(scale_table, task_ids)
    scaled_vecs = (
        jnp.concatenate([solves, probes, alpha_solve[None, :]], 0) * trial_scale[None, :]
    ).astype(jnp.bfloat16)

    def unpack(packed):
        return (packed[:feat_width], packed[feat_width:])

    payload = jnp.concatenate([feat_rows, scaled_vecs], 0)
    row_packed = lax.all_gather(payload, "cols", axis=1, tiled=True)
    row_feats, row_vecs = unpack(row_packed)
    row_count = row_feats.shape[1]
    empty = (jnp.zeros((feat_width, row_count), jnp.float32), jnp.zeros((row_count,), jnp.float32))
    shard_block = lax.all_gather(payload, "rows", axis=1, tiled=True)
    col_feats, col_vecs = unpack(shard_block)
    shard_count = shard_block.shape[1] // trial_count
    span_shards = math.gcd(shard_count, max(1, 512 // trial_count))
    block_cols = span_shards * trial_count

    def add_block(step_id, running):
        first_col = step_id * block_cols
        part_feats = lax.dynamic_slice_in_dim(col_feats, first_col, block_cols, 1)
        part_vecs = lax.dynamic_slice_in_dim(col_vecs, first_col, block_cols, 1)
        block_sum, block_weight = tile_terms(row_feats, row_vecs, part_feats, part_vecs)
        return (running[0] + block_sum, running[1] + block_weight)

    totals, weight_sum = lax.fori_loop(0, shard_count // span_shards, add_block, empty)
    local_grad = (totals - weight_sum[None, :] * row_feats.astype(jnp.float32)) * (
        2.0 * kernel_rate / feat_width
    )
    feat_grad = lax.psum_scatter(local_grad, "cols", scatter_dimension=1, tiled=True)
    grad_feats = feat_grad.astype(jnp.bfloat16)
    grad_hidden = jnp.dot(w_out, grad_feats, preferred_element_type=jnp.float32)
    sigmoid_pre = jax.nn.sigmoid(preact)
    grad_pre = grad_hidden * (sigmoid_pre * (1.0 + preact * (1.0 - sigmoid_pre)))
    grad_pre_b = grad_pre.astype(jnp.bfloat16)
    part_w_in = lax.dot_general(
        inputs, grad_pre_b, (((1,), (1,)), ((), ())), preferred_element_type=jnp.float32
    )
    part_b_in = jnp.sum(grad_pre, 1)
    part_w_out = lax.dot_general(
        hidden, grad_feats, (((1,), (1,)), ((), ())), preferred_element_type=jnp.float32
    )
    grad_w_in, grad_b_in, grad_w_out = lax.psum(
        (part_w_in, part_b_in, part_w_out), ("rows", "cols")
    )
    factor = 1.0 / math.sqrt(trial_count * lax.axis_size("rows") * lax.axis_size("cols"))
    return (feat_grad, grad_w_in * factor, grad_b_in * factor, grad_w_out * factor)


def solution(mesh):
    in_specs = (
        P(None, ("groups", "rows", "cols")),
        P(("groups", "rows", "cols")),
        P(),
        P(None, ("groups", "rows", "cols")),
        P(None, ("groups", "rows", "cols")),
        P(("groups", "rows", "cols")),
        P(),
        P(),
        P(),
    )
    out_specs = (
        P(None, ("groups", "rows", "cols")),
        P("groups", None),
        P("groups"),
        P("groups", None),
    )
    return jax.shard_map(body, mesh=mesh, in_specs=in_specs, out_specs=out_specs, check_vma=False)
```

profile of v0, /device:TPU:0, one launch (start us, length us, event | category | flops | bytes accessed | tf_op | source)
XLA Modules:
  0.0 212.7 jit_solution(5678300240845797002)
XLA Ops:
  7.2 0.0 copy-start
  7.2 0.0 copy-start.5
  7.2 0.0 copy-start.2
  7.2 0.0 copy-start.3
  7.2 0.0 reduce-scatter.4.cloned.1.call-start
  7.3 0.7 compare_select_fusion
  8.0 1.9 gather_fusion
  9.9 0.7 and_select_fusion
  10.6 1.0 multiply_convert_fusion
  11.6 0.0 copy-done
  11.6 0.1 fusion.20
  11.7 0.0 copy-done.5
  11.7 0.0 copy-done.2
  11.8 0.0 copy-done.3
  11.8 0.1 copy.21
  11.9 6.8 %all_gather.7 = bf16[97,768]{0,1:T(8,128)(2,1)S(1)} all-gather(bf16[97,192]{0,1:T(8,128)(2,1)S(1)} %copy.21), channel_id=1, replica_groups=mesh['groups'=2,'rows'=4,'cols'=4] {'cols'}, dimensions={1}, use_global_device_ids=true | all-gather | bytes 186240 | tf_op jit(solution)/shard_map/all_gather | solution.py:72
  18.8 14.0 %all_gather.6 = bf16[97,768]{0,1:T(8,128)(2,1)S(1)} all-gather(bf16[97,192]{0,1:T(8,128)(2,1)S(1)} %copy.21), channel_id=1, replica_groups=mesh['groups'=2,'rows'=4,'cols'=4] {'rows'}, dimensions={1}, use_global_device_ids=true | all-gather | bytes 186240 | tf_op jit(solution)/shard_map/all_gather | solution.py:76
  32.8 0.1 slice.60
  32.9 0.1 copy.29
  33.1 0.1 slice.59
  33.2 0.1 copy.25
  33.3 0.2 copy.26
  33.5 0.1 copy.24
  33.6 2.6 %while.16 = (s32[]{:T(128)}, f32[64,768]{1,0:T(8,128)S(1)}, f32[768]{0:T(1024)S(1)}, bf16[64,768]{1,0:T(8,128)(2,1)S(1)}, bf16[33,768]{1,0:T(8,128)(2,1)S(1)}, /...) while((s32[]{:T(128)}, f32[64,768]{1,0:T(8,128)S(1)}, ...), condition=%wide.region_4.5_spmd.clone, body=%wide.region_0.4_spmd.clone.sunk | while | flops 97985280 | bytes 4435434 | solution.py:89
  33.7 0.4 fusion.51
  34.2 0.4 fusion.54
  34.7 0.2 convolution_add_fusion.3
  35.0 0.4 fusion.51
  35.5 0.4 fusion.54
  36.0 0.2 convolution_add_fusion.3
  36.3 0.0 copy-start.4
  36.3 0.9 copy.27
  37.2 0.0 reduce-scatter.4.cloned.1.call-update
  37.2 0.0 all-reduce.3.cloned.1.call-start
  37.3 22.3 %reduce-scatter.4.cloned.1.call-done = f32[192,64]{1,0:T(8,128)} async-done(((f32[768,64]{1,0:T(8,128)}), f32[192,64]{1,0:T(8,128)}) %reduce-scatter.4.cloned.1.call-update) | async-done | bytes 49168
  59.6 1.0 copy.28
  60.6 0.0 copy-start.1
  60.6 0.8 fusion.23
  61.4 0.2 fusion.28
  61.6 0.0 copy-done.4
  61.6 0.1 convolution_bitcast_fusion.1
  61.7 60.3 %all-reduce = (f32[32,256]{1,0:T(8,128)S(1)}, f32[256]{0:T(256)S(1)}) all-reduce(f32[32,256]{1,0:T(8,128)S(1)} %convolution_bitcast_fusion.1, f32[256]{0:T(256)S(1)} %get-tuple-element.191), channel_id=1, replica_groups=mesh['groups'=2,'rows'=4,'cols'=4] {'rows','cols'}, use_global_device_ids=true, to_apply=%region_6.7 | all-reduce | flops 8448 | bytes 67584 | tf_op jit(solution)/shard_map/psum | solution.py:106
  122.0 0.6 broadcast_multiply_fusion.1
  122.6 0.0 all-reduce.3.cloned.1.call-update
  122.6 0.6 broadcast_multiply_fusion.2
  123.2 81.2 %all-reduce.3.cloned.1.call-done = f32[256,64]{0,1:T(8,128)} async-done(((f32[256,64]{0,1:T(8,128)}), f32[256,64]{0,1:T(8,128)}) %all-reduce.3.cloned.1.call-update) | async-done | bytes 65552 | tf_op jit(solution)/shard_map/psum | solution.py:106
  204.4 1.5 broadcast_multiply_fusion
  205.9 0.0 copy-done.1
  (18 shorter events, 0.3 us)
Async XLA Ops:
  7.2 4.4 %copy-start = (bf16[256,64]{0,1:T(8,128)(2,1)S(1)}, bf16[256,64]{0,1:T(8,128)(2,1)}, u32[]{:S(2)}) copy-start(bf16[256,64]{0,1:T(8,128)(2,1)} %param.19) | copy-start | bytes 98308
  7.2 4.5 %copy-start.5 = (f32[192]{0:T(256)S(1)}, f32[192]{0:T(256)}, u32[]{:S(2)}) copy-start(f32[192]{0:T(256)} %param.16) | copy-start | bytes 2308
  7.2 4.6 %copy-start.2 = (f32[16,192]{1,0:T(8,128)S(1)}, f32[16,192]{1,0:T(8,128)}, u32[]{:S(2)}) copy-start(f32[16,192]{1,0:T(8,128)} %param.14) | copy-start | bytes 36868
  7.2 4.6 %copy-start.3 = (f32[16,192]{1,0:T(8,128)S(1)}, f32[16,192]{1,0:T(8,128)}, u32[]{:S(2)}) copy-start(f32[16,192]{1,0:T(8,128)} %param.15) | copy-start | bytes 36868
  7.2 52.4 %reduce-scatter.4.cloned.1.call-start = ((), (), s32[]{:S(2)}) async-start(), calls=%async_computation.2 | async-start | bytes 491520
  36.3 25.3 %copy-start.4 = (bf16[32,192]{1,0:T(8,128)(2,1)S(1)}, bf16[32,192]{1,0:T(8,128)(2,1)}, u32[]{:S(2)}) copy-start(bf16[32,192]{1,0:T(8,128)(2,1)} %param.11) | copy-start | bytes 36868
  37.2 167.2 %all-reduce.3.cloned.1.call-start = ((), (), s32[]{:S(2)}) async-start(), calls=%async_computation.1 | async-start | bytes 131072 | tf_op jit(solution)/shard_map/psum | solution.py:106
  60.6 145.3 %copy-start.1 = (f32[64,192]{1,0:T(8,128)}, f32[64,192]{1,0:T(8,128)S(1)}, u32[]{:S(2)}) copy-start(f32[64,192]{1,0:T(8,128)S(1)} %copy.28) | copy-start | bytes 147460
Sparse Core Ops, SparseCore 0:
  37.3 22.1 reduce-scatter.3
  122.8 81.5 all-reduce.2
where the time goes:
time: 214 us; the launch traced here: 213 us
  waiting for transfers between devices  104 us (49%)
  blocking collectives  81.1 us (38%)
  between operations  14.2 us (7%)
  local copies, waits for them, and re-layouts  4.83 us (2%)
  matrix products  4.46 us (2%)
  other arithmetic  4.33 us (2%)
    psum x1, waiting for transfers between devices, body(): lax.psum((part_w_in, part_b_in, part_w_out), ('rows', 'cols'))  81.2 us
    psum x1, blocking collectives, body(): lax.psum((part_w_in, part_b_in, part_w_out), ('rows', 'cols'))  60.3 us
    unnamed x3, waiting for transfers between devices  22.3 us
    all_gather x1, blocking collectives, body(): shard_block = lax.all_gather(payload, 'rows', axis=1, tiled=True)  14 us
    all_gather x1, blocking collectives, body(): row_packed = lax.all_gather(payload, 'cols', axis=1, tiled=True)  6.84 us
  transfers between devices with their start and end apart: 2, of which 2 were waited for; matrix products, arithmetic and copies ran while one was open for 0% of the time, Pallas kernels for 0%

commit v1 on v0

v1 whole, which is shorter than its diff:
```python
import functools
import math

import jax
import jax.numpy as jnp
from jax import lax
from jax.experimental import pallas as pl
from jax.experimental.pallas import tpu as pltpu
from jax.sharding import PartitionSpec as P

kernel_rate = 1.0
MESH = pl.DeviceIdType.MESH
LANES = 128


def split3(value):
    high = value.astype(jnp.bfloat16).astype(jnp.float32)
    rest = value - high
    mid = rest.astype(jnp.bfloat16).astype(jnp.float32)
    low = (rest - mid).astype(jnp.bfloat16).astype(jnp.float32)
    return high, mid, low


def whole_kernel(
    R, C,
    inputs_ref, ids_ref, table_ref, probes_ref, solves_ref, alpha_ref, w_in_ref, b_in_ref, w_out_ref,
    fgrad_ref, gw_in_ref, gb_in_ref, gw_out_ref,
    buf, parts, rs_buf, ag_buf, ag_size,
    recv_sem, send_sem, rs_send, rs_recv, ag_send, ag_recv,
):
    n = R * C
    r, c = lax.axis_index("rows"), lax.axis_index("cols")
    me = r * C + c
    trials = inputs_ref.shape[1]
    feat_width = w_out_ref.shape[1]
    probe_count = probes_ref.shape[0]
    pieces = parts.shape[0]

    def coords(q):
        return {"rows": q // C, "cols": lax.rem(q, C)}

    def other(k):
        return lax.rem(me + k, n)

    barrier = pltpu.get_barrier_semaphore()

    @pl.loop(1, n)
    def _(k):
        pl.semaphore_signal(barrier, inc=1, device_id=coords(other(k)), device_id_type=MESH)

    inputs = inputs_ref[...]
    preact = lax.dot_general(
        inputs, w_in_ref[...], (((0,), (0,)), ((), ())), preferred_element_type=jnp.float32
    ) + b_in_ref[...]
    sig = 1.0 / (1.0 + jnp.exp(-preact))
    hidden = (preact * sig).astype(jnp.bfloat16)
    feats = jnp.dot(hidden, w_out_ref[...], preferred_element_type=jnp.float32).astype(jnp.bfloat16)
    feats_f = feats.astype(jnp.float32)
    sqnorm = jnp.sum(feats_f * feats_f, 1, keepdims=True)

    ids = ids_ref[...]
    lo, hi = lax.rem(ids, LANES), ids // LANES
    table = table_ref[...]
    groups = table.shape[0]
    hot = (lax.broadcasted_iota(jnp.int32, (LANES, trials), 0) == lo).astype(jnp.float32).astype(jnp.bfloat16)
    terms = jnp.concatenate(split3(table), 0).astype(jnp.bfloat16)
    found = jnp.dot(terms, hot, preferred_element_type=jnp.float32)
    found = found[:groups] + found[groups : 2 * groups] + found[2 * groups :]
    mine = lax.broadcasted_iota(jnp.int32, (groups, trials), 0) == hi
    scale = jnp.sum(jnp.where(mine, found, 0.0), 0, keepdims=True)

    vec_rows = LANES - feat_width
    vecs = jnp.concatenate(
        [
            solves_ref[...] * scale,
            probes_ref[...] * scale,
            jnp.broadcast_to(alpha_ref[...] * scale, (vec_rows - 2 * probe_count, trials)),
        ],
        0,
    )
    pad = -trials % LANES
    vecs = jnp.concatenate([vecs, jnp.zeros((vec_rows, pad), jnp.float32)], 1)
    vecs = jnp.transpose(vecs)[:trials].astype(jnp.bfloat16).astype(jnp.float32)

    first_u, first_z = feat_width, feat_width + probe_count
    at_a = feat_width + 2 * probe_count
    lane = lax.broadcasted_iota(jnp.int32, (trials, LANES), 1)
    n_hi, n_mid, n_lo = split3(sqnorm)
    base = jnp.concatenate([feats_f, vecs], 1)
    payload = jnp.where(
        lane <= at_a,
        base,
        jnp.where(
            lane == at_a + 1, n_hi,
            jnp.where(
                lane == at_a + 2, n_mid,
                jnp.where(lane == at_a + 3, n_lo, jnp.where(lane <= at_a + 6, 1.0, 0.0)),
            ),
        ),
    )
    buf[c * R + r] = payload.astype(jnp.bfloat16)

    rate = kernel_rate / feat_width
    row_exp = jnp.where(
        lane < feat_width,
        base * (2.0 * rate),
        jnp.where(
            lane <= at_a, 0.0,
            jnp.where(
                lane <= at_a + 3, -rate,
                jnp.where(
                    lane == at_a + 4, n_hi * -rate,
                    jnp.where(
                        lane == at_a + 5, n_mid * -rate,
                        jnp.where(lane == at_a + 6, n_lo * -rate, 0.0),
                    ),
                ),
            ),
        ),
    )
    swapped = jnp.concatenate(
        [feats_f, vecs[:, probe_count : 2 * probe_count], vecs[:, :probe_count], vecs[:, 2 * probe_count :]], 1
    )
    row_pair = jnp.where(
        lane < feat_width, 0.0,
        jnp.where(lane < at_a, swapped * (0.5 / probe_count), jnp.where(lane == at_a, -swapped, 0.0)),
    )
    left = jnp.concatenate([row_exp, row_pair], 0).astype(jnp.bfloat16)

    pl.semaphore_wait(barrier, n - 1)

    def copy(slot, device):
        return pltpu.make_async_remote_copy(
            src_ref=buf.at[slot], dst_ref=buf.at[slot], send_sem=send_sem, recv_sem=recv_sem.at[slot],
            device_id=device, device_id_type=MESH,
        )

    def wait_slot(slot):
        pltpu.make_async_copy(buf.at[slot], buf.at[slot], recv_sem.at[slot]).wait()

    bits = []
    while (1 << len(bits)) < C:
        bits.insert(0, 1 << len(bits))

    def forward(mask, slot):
        for bit in bits:
            if mask == 0 or bit < (mask & -mask):
                copy(slot, {"rows": r, "cols": c ^ bit}).start()

    def compute(mask, carry):
        group = c ^ mask

        def pair_step(step, carry):
            total, sums = carry
            cols = buf[pl.ds(group * R + 2 * step, 2)].reshape(2 * trials, LANES)
            both = lax.dot_general(left, cols, (((1,), (1,)), ((), ())), preferred_element_type=jnp.float32)
            weight = both[trials:] * jnp.exp(both[:trials])
            for k in range(2 * trials // LANES):
                sums = sums + weight[:, k * LANES : (k + 1) * LANES]
            total = total + jnp.dot(weight.astype(jnp.bfloat16), cols, preferred_element_type=jnp.float32)
            return total, sums

        return lax.fori_loop(0, R // 2, pair_step, carry)

    own = c * R + r

    @pl.loop(1, R)
    def _(k):
        copy(own, {"rows": lax.rem(r + k, R), "cols": c}).start()

    forward(0, own)

    @pl.loop(1, R)
    def _(k):
        slot = c * R + lax.rem(r + k, R)
        wait_slot(slot)
        forward(0, slot)

    empty = jnp.zeros((trials, LANES), jnp.float32)
    carry = compute(0, (empty, empty))
    masks = sorted(range(1, C), key=lambda m: (-(m & -m), m))
    for mask in masks:
        @pl.loop(0, R)
        def _(k):
            slot = (c ^ mask) * R + lax.rem(r + k, R)
            wait_slot(slot)
            forward(mask, slot)

        carry = compute(mask, carry)
    total, sums = carry

    weight_sum = jnp.sum(sums, 1, keepdims=True)
    feat_grad = (total[:, :feat_width] - weight_sum * feats_f) * (2.0 * rate)
    grad_feats = feat_grad.astype(jnp.bfloat16)
    grad_hidden = lax.dot_general(
        grad_feats, w_out_ref[...], (((1,), (1,)), ((), ())), preferred_element_type=jnp.float32
    )
    grad_pre = grad_hidden * (sig * (1.0 + preact * (1.0 - sig)))
    g_in = jnp.dot(inputs, grad_pre.astype(jnp.bfloat16), preferred_element_type=jnp.float32)
    g_out = lax.dot_general(
        grad_feats, hidden, (((0,), (0,)), ((), ())), preferred_element_type=jnp.float32
    )
    g_bias = jnp.broadcast_to(jnp.sum(grad_pre, 0, keepdims=True), (8, grad_pre.shape[1]))
    packed = jnp.concatenate([g_in, g_out, g_bias], 0)
    for p in range(pieces):
        for h in range(2):
            parts[p, 8 * h : 8 * h + 8] = packed[8 * p : 8 * p + 8, h * LANES : (h + 1) * LANES]

    def piece_copy(p):
        return pltpu.make_async_remote_copy(
            src_ref=parts.at[p], dst_ref=rs_buf.at[me], send_sem=rs_send.at[p], recv_sem=rs_recv,
            device_id=coords(p), device_id_type=MESH,
        )

    @pl.loop(0, pieces)
    def _(k):
        p = lax.rem(me + k, pieces)

        @pl.when(p != me)
        def _():
            piece_copy(p).start()

    wide = jnp.concatenate([feat_grad, jnp.zeros((trials, LANES - feat_width), jnp.float32)], 1)
    wide = jnp.concatenate([wide, jnp.zeros((pad, LANES), jnp.float32)], 0)
    fgrad_ref[...] = jnp.transpose(wide)[:feat_width, :trials]

    def ag_copy(k):
        return pltpu.make_async_remote_copy(
            src_ref=ag_buf.at[me], dst_ref=ag_buf.at[me], send_sem=ag_send, recv_sem=ag_recv,
            device_id=coords(other(k)), device_id_type=MESH,
        )

    factor = 1.0 / math.sqrt(trials * n)

    @pl.when(me < pieces)
    def _():
        rs_buf[me] = parts[me]
        pltpu.make_async_copy(rs_buf.at[pl.ds(0, n - 1)], rs_buf.at[pl.ds(0, n - 1)], rs_recv).wait()
        summed = jnp.sum(rs_buf[...], 0) * factor
        ag_buf[me] = summed.astype(jnp.bfloat16)

        @pl.loop(1, n)
        def _(k):
            ag_copy(k).start()

        view = ag_buf.at[pl.ds(0, pieces - 1)]
        pltpu.make_async_copy(view, view, ag_recv).wait()

    @pl.when(me >= pieces)
    def _():
        pltpu.make_async_copy(ag_buf, ag_buf, ag_recv).wait()

    def unpack(first, count):
        rows = []
        for p in range(first, first + count):
            piece = ag_buf[p].astype(jnp.float32)
            rows.append(jnp.concatenate([piece[:8], piece[8:]], 1))
        return jnp.concatenate(rows, 0) if count > 1 else rows[0]

    in_pieces, out_pieces = g_in.shape[0] // 8, feat_width // 8
    gw_in_ref[...] = unpack(0, in_pieces)
    gw_out_ref[...] = unpack(in_pieces, out_pieces)
    gb_in_ref[...] = unpack(in_pieces + out_pieces, 1)[:1]

    pltpu.make_async_copy(buf.at[pl.ds(0, n - 1)], buf.at[pl.ds(0, n - 1)], send_sem).wait()

    @pl.loop(0, pieces)
    def _(p):
        @pl.when(p != me)
        def _():
            piece_copy(p).wait_send()

    @pl.when(me < pieces)
    def _():
        pltpu.make_async_copy(ag_size, ag_size, ag_send).wait()


def solution(mesh):
    R, C = mesh.shape["rows"], mesh.shape["cols"]
    n = R * C

    def body(inputs, task_ids, scale_table, probes, solves, alpha_solve, w_in, b_in, w_out):
        width, trials = inputs.shape
        hidden_width, feat_width = w_out.shape
        pieces = (width + feat_width) // 8 + 1
        tasks = scale_table.shape[0]
        table = jnp.pad(scale_table, (0, -tasks % (8 * LANES))).reshape(-1, LANES)
        vmem = pl.BlockSpec(memory_space=pltpu.VMEM)
        fgrad, gw_in, gb_in, gw_out = pl.pallas_call(
            functools.partial(whole_kernel, R, C),
            out_shape=(
                jax.ShapeDtypeStruct((feat_width, trials), jnp.float32),
                jax.ShapeDtypeStruct((width, hidden_width), jnp.float32),
                jax.ShapeDtypeStruct((1, hidden_width), jnp.float32),
                jax.ShapeDtypeStruct((feat_width, hidden_width), jnp.float32),
            ),
            in_specs=[vmem] * 9,
            out_specs=(vmem,) * 4,
            scratch_shapes=[
                pltpu.VMEM((n, trials, LANES), jnp.bfloat16),
                pltpu.VMEM((pieces, 16, LANES), jnp.float32),
                pltpu.VMEM((n, 16, LANES), jnp.float32),
                pltpu.VMEM((pieces, 16, LANES), jnp.bfloat16),
                pltpu.VMEM((n - 1, 16, LANES), jnp.bfloat16),
                pltpu.SemaphoreType.DMA((n,)),
                pltpu.SemaphoreType.DMA,
                pltpu.SemaphoreType.DMA((pieces,)),
                pltpu.SemaphoreType.DMA,
                pltpu.SemaphoreType.DMA,
                pltpu.SemaphoreType.DMA,
            ],
            compiler_params=pltpu.CompilerParams(
                collective_id=0, has_side_effects=True, vmem_limit_bytes=48 * 1024 * 1024
            ),
        )(
            inputs, task_ids[None, :], table, probes, solves, alpha_solve[None, :], w_in, b_in[None, :], w_out
        )
        return fgrad, gw_in, gb_in[0], jnp.transpose(gw_out)

    split = ("groups", "rows", "cols")
    return jax.shard_map(
        body,
        mesh=mesh,
        in_specs=(
            P(None, split), P(split), P(), P(None, split), P(None, split), P(split), P(), P(), P(),
        ),
        out_specs=(P(None, split), P("groups", None), P("groups"), P("groups", None)),
        check_vma=False,
    )
```

time: 214 us -> 32.6 us (0.15)
  waiting for transfers between devices: 104 us -> 0 us
  blocking collectives: 81.1 us -> 0 us
  Pallas kernels: 0 us -> 27.5 us
  between operations: 14.2 us -> 0.73 us
  matrix products: 4.46 us -> 0 us
  other arithmetic: 4.33 us -> 0 us
    psum x1 -> x0, waiting for transfers between devices: 81.2 us -> none  [body(): lax.psum((part_w_in, part_b_in, part_w_out), ('rows', 'cols'))]
    psum x1 -> x0, blocking collectives: 60.3 us -> none  [body(): lax.psum((part_w_in, part_b_in, part_w_out), ('rows', 'cols'))]
    pallas_call x0 -> x1, Pallas kernels: none -> 27.5 us  [body(): pl.pallas_call(functools.partial(whole_kernel, R, C), out_shape=(jax.Shap...]
    unnamed x3 -> x0, waiting for transfers between devices: 22.3 us -> none
    all_gather x2 -> x0, blocking collectives: 20.9 us -> none  [the longest x1 14 us: body(): shard_block = lax.all_gather(payload, 'rows', axis=1, tiled=True)]
    dot_general x11 -> x0, matrix products: 4.46 us -> none  [the longest x1 0.98 us: project(): lax.dot_general(w_in, inputs, (((0,), (0,)), ((), ())), preferred_element...]
    mul x6 -> x0, other arithmetic: 2.75 us -> none  [the longest x1 1.47 us: body(): grad_w_out * factor]
  transfers between devices with their start and end apart: 2 -> 0, of which waited for: 2 -> 0; matrix products, arithmetic and copies ran while one was open for 0% -> 0% of each run, Pallas kernels for 0% -> 0%
where the time goes in v1:
time: 32.6 us; the launch traced here: 32.4 us
  Pallas kernels  27.5 us (84%)
  local copies, waits for them, and re-layouts  4.11 us (13%)
  between operations  0.73 us (2%)
    pallas_call x1, Pallas kernels, body(): pl.pallas_call(functools.partial(whole_kernel, R, C), out_shape=(jax.Shap...  27.5 us
    unnamed x19, local copies, waits for them, and re-layouts  3.4 us
    reshape x1, local copies, waits for them, and re-layouts, body(): table = jnp.pad(scale_table, (0, -tasks % (8 * LANES))).reshape(-1, LANES)  0.71 us

profile of v1, /device:TPU:0, one launch (start us, length us, event | category | flops | bytes accessed | tf_op | source)
XLA Modules:
  0.0 32.4 jit_solution(15459746711124142195)
XLA Ops:
  0.6 0.7 %pad_bitcast_fusion.table_ref = f32[24,128]{1,0:T(8,128)S(1)} fusion(f32[3000]{0:T(1024)} %param.11), kind=kLoop, calls=%fused_computation | loop fusion | bytes 24288 | tf_op jit(solution)/shard_map/reshape | solution.py:287
  1.3 0.0 copy-start
  1.3 0.0 copy-start.1
  1.3 0.0 copy-start.2
  1.4 0.0 copy-start.3
  1.4 0.0 copy-start.4
  1.4 0.0 copy-start.5
  1.4 0.0 copy-start.6
  1.4 0.9 %copy.13.w_out_ref = bf16[256,64]{1,0:T(8,128)(2,1)S(1)} copy(bf16[256,64]{0,1:T(8,128)(2,1)} %param.17) | data formatting | bytes 65536 | tf_op args[8]
  2.3 0.0 copy-done
  2.3 0.0 copy-done.1
  2.3 0.0 copy-done.2
  2.4 0.0 copy-done.3
  2.4 0.0 copy-done.4
  2.4 0.0 copy-done.5
  2.4 0.0 copy-done.6
  2.4 27.5 %shard_map.120 = (f32[64,192]{1,0:T(8,128)S(1)}, f32[32,256]{1,0:T(8,128)S(1)}, f32[1,256]{1,0:T(1,128)S(1)}, f32[64,256]{1,0:T(8,128)S(1)}) custom-call(bf16[32,192]{1,0:T(8,128)(2,1)S(1)} %copy-done, s32[1,192]{1,0:T(1,128)S(1)} %bitcast.8, f32[24,128]{1,0:T(8,128)S(1)} %pad_bitcast_fusion.table_ref, f32[16,192]{1,0:T(8,128)S(1)} %copy-done.1, ...), custom_call_target="tpu_custom_call" | custom-call | tf_op jit(solution)/shard_map/pallas_call | solution.py:289
  29.9 0.6 %copy.18 = f32[64,192]{1,0:T(8,128)} copy(f32[64,192]{1,0:T(8,128)S(1)} %get-tuple-element.16) | data formatting | bytes 98304
  30.5 0.6 %copy.19 = f32[32,256]{1,0:T(8,128)} copy(f32[32,256]{1,0:T(8,128)S(1)} %get-tuple-element.17) | data formatting | bytes 65536
  31.2 0.6 %copy.20 = f32[256]{0:T(256)} copy(f32[256]{0:T(256)S(1)} %bitcast.11) | data formatting | bytes 2048
  31.7 0.6 %copy.21 = f32[256,64]{0,1:T(8,128)} copy(f32[256,64]{0,1:T(8,128)S(1)} %bitcast.7) | data formatting | bytes 131072
Async XLA Ops:
  1.3 1.0 %copy-start = (bf16[32,192]{1,0:T(8,128)(2,1)S(1)}, bf16[32,192]{1,0:T(8,128)(2,1)}, u32[]{:S(2)}) copy-start(bf16[32,192]{1,0:T(8,128)(2,1)} %inputs_ref.1) | copy-start | bytes 36868
  1.3 1.0 %copy-start.1 = (f32[16,192]{1,0:T(8,128)S(1)}, f32[16,192]{1,0:T(8,128)}, u32[]{:S(2)}) copy-start(f32[16,192]{1,0:T(8,128)} %probes_ref.1) | copy-start | bytes 36868
  1.3 1.0 %copy-start.2 = (f32[16,192]{1,0:T(8,128)S(1)}, f32[16,192]{1,0:T(8,128)}, u32[]{:S(2)}) copy-start(f32[16,192]{1,0:T(8,128)} %solves_ref.1) | copy-start | bytes 36868
  1.4 1.0 %copy-start.3 = (bf16[32,256]{1,0:T(8,128)(2,1)S(1)}, bf16[32,256]{1,0:T(8,128)(2,1)}, u32[]{:S(2)}) copy-start(bf16[32,256]{1,0:T(8,128)(2,1)} %w_in_ref.1) | copy-start | bytes 49156
  1.4 1.0 %copy-start.4 = (s32[192]{0:T(256)S(1)}, s32[192]{0:T(256)}, u32[]{:S(2)}) copy-start(s32[192]{0:T(256)} %param.10) | copy-start | bytes 2308
  1.4 1.0 %copy-start.5 = (f32[192]{0:T(256)S(1)}, f32[192]{0:T(256)}, u32[]{:S(2)}) copy-start(f32[192]{0:T(256)} %param.14) | copy-start | bytes 2308
  1.4 1.0 %copy-start.6 = (f32[256]{0:T(256)S(1)}, f32[256]{0:T(256)}, u32[]{:S(2)}) copy-start(f32[256]{0:T(256)} %param.16) | copy-start | bytes 3076

commit v2 on v1

v2 whole, which is shorter than its diff:
```python
import functools
import math

import jax
import jax.numpy as jnp
from jax import lax
from jax.experimental import pallas as pl
from jax.experimental.pallas import tpu as pltpu
from jax.sharding import PartitionSpec as P

kernel_rate = 1.0
MESH = pl.DeviceIdType.MESH
LANES = 128


def split3(value):
    high = value.astype(jnp.bfloat16).astype(jnp.float32)
    rest = value - high
    mid = rest.astype(jnp.bfloat16).astype(jnp.float32)
    low = (rest - mid).astype(jnp.bfloat16).astype(jnp.float32)
    return high, mid, low


def whole_kernel(
    R, C,
    *refs_and_scratch,
):
    operands, refs = refs_and_scratch[:9], refs_and_scratch[9:]
    fgrad_ref, sums_ref, *refs = refs
    staged, (load_sem, *refs) = refs[:9], refs[9:]
    inputs_ref, ids_ref, table_ref, probes_ref, solves_ref, alpha_ref, w_in_ref, b_in_ref, w_out_t_ref = staged
    (
        buf, left_buf, swap, parts, rs_buf, ag_buf, ag_size,
        recv_sem, send_sem, core_send, core_recv, rs_send, rs_recv, ag_send, ag_recv,
    ) = refs
    n = R * C
    r, c = lax.axis_index("rows"), lax.axis_index("cols")
    me = r * C + c
    trials = inputs_ref.shape[1]
    feat_width = w_out_t_ref.shape[0]
    probe_count = probes_ref.shape[0]
    pieces = parts.shape[0]

    def coords(q):
        return {"rows": q // C, "cols": lax.rem(q, C)}

    def other(k):
        return lax.rem(me + k, n)

    barrier = pltpu.get_barrier_semaphore()

    @pl.loop(1, n)
    def _(k):
        pl.semaphore_signal(barrier, inc=1, device_id=coords(other(k)), device_id_type=MESH)

    loads = [
        pltpu.make_async_copy(operands[k], staged[k], load_sem.at[k]) for k in range(9)
    ]
    for load in loads:
        load.start()

    for load in loads:
        load.wait()

    ids = ids_ref[...]
    lo, hi = lax.rem(ids, LANES), ids // LANES
    flat = table_ref[...]
    tasks = flat.shape[1]
    groups = -(-tasks // (8 * LANES)) * 8
    flat = jnp.concatenate([flat, jnp.zeros((1, groups * LANES - tasks), jnp.float32)], 1)
    table = jnp.concatenate([flat[:, k * LANES : (k + 1) * LANES] for k in range(groups)], 0)
    hot = (lax.broadcasted_iota(jnp.int32, (LANES, trials), 0) == lo).astype(jnp.float32).astype(jnp.bfloat16)
    terms = jnp.concatenate(split3(table), 0).astype(jnp.bfloat16)
    found = jnp.dot(terms, hot, preferred_element_type=jnp.float32)
    found = found[:groups] + found[groups : 2 * groups] + found[2 * groups :]
    mine = lax.broadcasted_iota(jnp.int32, (groups, trials), 0) == hi
    scale = jnp.sum(jnp.where(mine, found, 0.0), 0, keepdims=True)

    inputs = inputs_ref[...]
    width, half = inputs.shape[0], trials // 2
    raw_lanes = width + 2 * probe_count
    pad = -trials % LANES
    raw = jnp.concatenate(
        [
            inputs.astype(jnp.float32),
            solves_ref[...] * scale,
            probes_ref[...] * scale,
            jnp.broadcast_to(alpha_ref[...] * scale, (LANES - raw_lanes, trials)),
        ],
        0,
    )
    raw = jnp.transpose(jnp.concatenate([raw, jnp.zeros((LANES, pad), jnp.float32)], 1))[:trials]
    raw = raw.astype(jnp.bfloat16).astype(jnp.float32)

    chips = n // 2
    here, side = r * (C // 2) + c // 2, lax.rem(c, 2)
    main_part = jnp.concatenate([raw[:half, :raw_lanes], raw[half:, :raw_lanes]], 1)
    tile_lane = lax.broadcasted_iota(jnp.int32, (16, LANES), 1)
    a_part = jnp.zeros((16, LANES), jnp.float32)
    for k in range(trials // 16):
        a_part = jnp.where(tile_lane == k, raw[16 * k : 16 * k + 16, raw_lanes : raw_lanes + 1], a_part)
    buf[here, :half] = main_part.astype(jnp.bfloat16)
    buf[here, half:] = a_part.astype(jnp.bfloat16)

    pl.semaphore_wait(barrier, n - 1)

    def send(k):
        chip = here ^ k
        pltpu.make_async_remote_copy(
            src_ref=buf.at[here], dst_ref=buf.at[here], send_sem=send_sem, recv_sem=recv_sem.at[here],
            device_id={"rows": chip // (C // 2), "cols": lax.rem(chip, C // 2) * 2 + side},
            device_id_type=MESH,
        ).start()

    far = chips // 2

    @pl.loop(far, chips)
    def _(k):
        send(k)

    @pl.loop(1, far)
    def _(k):
        send(k)

    w_in, b_in = w_in_ref[...], b_in_ref[...]
    hidden_width = w_in.shape[1]
    preact = lax.dot_general(
        inputs, w_in, (((0,), (0,)), ((), ())), preferred_element_type=jnp.float32
    ) + b_in
    sig = 1.0 / (1.0 + jnp.exp(-preact))
    hidden = (preact * sig).astype(jnp.bfloat16)
    w_out_t = w_out_t_ref[...]
    feats = lax.dot_general(
        hidden, w_out_t, (((1,), (1,)), ((), ())), preferred_element_type=jnp.float32
    ).astype(jnp.bfloat16)
    feats_f = feats.astype(jnp.float32)
    sqnorm = jnp.sum(feats_f * feats_f, 1, keepdims=True)
    vecs = raw[:, width : width + LANES - feat_width]

    first_u, first_z = feat_width, feat_width + probe_count
    at_a = feat_width + 2 * probe_count
    lane = lax.broadcasted_iota(jnp.int32, (trials, LANES), 1)
    n_hi, n_mid, n_lo = split3(sqnorm)
    base = jnp.concatenate([feats_f, vecs], 1)
    rate = kernel_rate / feat_width
    row_exp = jnp.where(
        lane < feat_width,
        base * (2.0 * rate),
        jnp.where(
            lane <= at_a, 0.0,
            jnp.where(
                lane <= at_a + 3, -rate,
                jnp.where(
                    lane == at_a + 4, n_hi * -rate,
                    jnp.where(
                        lane == at_a + 5, n_mid * -rate,
                        jnp.where(lane == at_a + 6, n_lo * -rate, 0.0),
                    ),
                ),
            ),
        ),
    )
    swapped = jnp.concatenate(
        [feats_f, vecs[:, probe_count : 2 * probe_count], vecs[:, :probe_count], vecs[:, 2 * probe_count :]], 1
    )
    row_pair = jnp.where(
        lane < feat_width, 0.0,
        jnp.where(lane < at_a, swapped * (0.5 / probe_count), jnp.where(lane == at_a, -swapped, 0.0)),
    )
    left_buf[0, 0] = row_exp.astype(jnp.bfloat16)
    left_buf[0, 1] = row_pair.astype(jnp.bfloat16)

    def core_copy(refs, which):
        return pltpu.make_async_remote_copy(
            src_ref=refs.at[0], dst_ref=refs.at[1], send_sem=core_send.at[which], recv_sem=core_recv.at[which],
            device_id={"rows": r, "cols": c ^ 1}, device_id_type=MESH,
        )

    def wait_chip(k):
        chip = here ^ k
        pltpu.make_async_copy(buf.at[chip], buf.at[chip], recv_sem.at[chip]).wait()

    core_copy(left_buf, 0).start()
    core_copy(left_buf, 0).wait()
    left = jnp.concatenate([left_buf[0, 0], left_buf[1, 0], left_buf[0, 1], left_buf[1, 1]], 0)

    blank = jnp.zeros((width, hidden_width), jnp.bfloat16)
    gap = jnp.zeros((2 * probe_count, 2 * hidden_width), jnp.bfloat16)
    first_layer = jnp.concatenate(
        [
            jnp.concatenate([w_in, blank], 1),
            gap,
            jnp.concatenate([blank, w_in], 1),
            gap,
        ],
        0,
    )
    bias = jnp.concatenate([b_in, b_in], 1)
    second_layer = jnp.concatenate([w_out_t, jnp.zeros((LANES - feat_width, hidden_width), jnp.bfloat16)], 0)
    s_row = lax.broadcasted_iota(jnp.int32, (2 * LANES, LANES), 0)
    s_lane = lax.broadcasted_iota(jnp.int32, (2 * LANES, LANES), 1)
    lane2 = lax.broadcasted_iota(jnp.int32, (trials, LANES), 1)
    block = lax.rem(lax.broadcasted_iota(jnp.int32, (trials, LANES), 0), half) // 16
    places, a_masks = [], []
    for h in range(2):
        vec_place = (s_row == s_lane - feat_width + width + h * raw_lanes) & (s_lane >= feat_width) & (s_lane < at_a)
        place = vec_place | ((s_row >= LANES) & (s_lane == at_a))
        places.append(place.astype(jnp.float32).astype(jnp.bfloat16))
        a_masks.append((lane2 == block + h * (half // 16)).astype(jnp.float32).astype(jnp.bfloat16))

    def columns(pair):
        blocks = buf[pl.ds(2 * pair, 2)]
        main = blocks[:, :half].reshape(trials, LANES)
        tiles = jnp.concatenate([blocks[0, half:]] * (half // 16) + [blocks[1, half:]] * (half // 16), 0)
        pre = jnp.dot(main, first_layer, preferred_element_type=jnp.float32) + bias
        hid = (pre * (1.0 / (1.0 + jnp.exp(-pre)))).astype(jnp.bfloat16)
        found = []
        for h in range(2):
            value = lax.dot_general(
                hid[:, h * hidden_width : (h + 1) * hidden_width], second_layer,
                (((1,), (1,)), ((), ())), preferred_element_type=jnp.float32,
            ) + jnp.dot(
                jnp.concatenate([main, tiles * a_masks[h]], 1), places[h], preferred_element_type=jnp.float32
            )
            value = value.astype(jnp.bfloat16).astype(jnp.float32)
            norm = jnp.sum(jnp.where(lane2 < feat_width, value * value, 0.0), 1, keepdims=True)
            high, mid, low = split3(norm)
            found.append(
                jnp.where(
                    lane2 <= at_a, value,
                    jnp.where(
                        lane2 == at_a + 1, high,
                        jnp.where(
                            lane2 == at_a + 2, mid,
                            jnp.where(lane2 == at_a + 3, low, jnp.where(lane2 <= at_a + 6, 1.0, 0.0)),
                        ),
                    ),
                )
            )
        return jnp.concatenate(found, 0).astype(jnp.bfloat16)

    def add_pair(p, carry):
        total, sums = carry
        cols = columns((here // 2) ^ p)
        both = lax.dot_general(left, cols, (((1,), (1,)), ((), ())), preferred_element_type=jnp.float32)
        weight = both[2 * trials :] * jnp.exp(both[: 2 * trials])
        for j in range(2 * trials // LANES):
            sums = sums + weight[:, j * LANES : (j + 1) * LANES]
        total = total + jnp.dot(weight.astype(jnp.bfloat16), cols, preferred_element_type=jnp.float32)
        return total, sums

    def step(p, carry):
        wait_chip(2 * p)
        wait_chip(2 * p + 1)
        return add_pair(p, carry)

    empty = jnp.zeros((2 * trials, LANES), jnp.float32)
    wait_chip(1)
    carry = add_pair(0, (empty, empty))
    total, sums = lax.fori_loop(1, chips // 2, step, carry)

    weight_sum = jnp.sum(sums, 1, keepdims=True)
    lane4 = lax.broadcasted_iota(jnp.int32, (2 * trials, LANES), 1)
    mixed = jnp.where(lane4 < feat_width, total, weight_sum)
    swap[0] = mixed[trials:]
    core_copy(swap, 1).start()
    core_copy(swap, 1).wait()
    mixed = mixed[:trials] + swap[1]
    total, weight_sum = mixed[:, :feat_width], mixed[:, feat_width : feat_width + 1]
    feat_grad = (total - weight_sum * feats_f) * (2.0 * rate)
    grad_feats = feat_grad.astype(jnp.bfloat16)
    grad_hidden = jnp.dot(grad_feats, w_out_t, preferred_element_type=jnp.float32)
    grad_pre = grad_hidden * (sig * (1.0 + preact * (1.0 - sig)))
    g_in = jnp.dot(inputs, grad_pre.astype(jnp.bfloat16), preferred_element_type=jnp.float32)
    g_out = lax.dot_general(
        grad_feats, hidden, (((0,), (0,)), ((), ())), preferred_element_type=jnp.float32
    )
    g_bias = jnp.broadcast_to(jnp.sum(grad_pre, 0, keepdims=True), (8, grad_pre.shape[1]))
    packed = jnp.concatenate([g_in, g_out, g_bias], 0)
    for p in range(pieces):
        for h in range(2):
            parts[p, 8 * h : 8 * h + 8] = packed[8 * p : 8 * p + 8, h * LANES : (h + 1) * LANES]

    def piece_copy(p):
        return pltpu.make_async_remote_copy(
            src_ref=parts.at[p], dst_ref=rs_buf.at[me], send_sem=rs_send.at[p], recv_sem=rs_recv,
            device_id=coords(p), device_id_type=MESH,
        )

    @pl.loop(0, pieces)
    def _(k):
        p = lax.rem(me + k, pieces)

        @pl.when(p != me)
        def _():
            piece_copy(p).start()

    wide = jnp.concatenate([feat_grad, jnp.zeros((trials, LANES - feat_width), jnp.float32)], 1)
    wide = jnp.concatenate([wide, jnp.zeros((pad, LANES), jnp.float32)], 0)
    fgrad_ref[...] = jnp.transpose(wide)[:feat_width, :trials]

    def ag_copy(k):
        return pltpu.make_async_remote_copy(
            src_ref=ag_buf.at[me], dst_ref=ag_buf.at[me], send_sem=ag_send, recv_sem=ag_recv,
            device_id=coords(other(k)), device_id_type=MESH,
        )

    factor = 1.0 / math.sqrt(trials * n)

    @pl.when(me < pieces)
    def _():
        rs_buf[me] = parts[me]
        pltpu.make_async_copy(rs_buf.at[pl.ds(0, n - 1)], rs_buf.at[pl.ds(0, n - 1)], rs_recv).wait()
        summed = jnp.sum(rs_buf[...], 0) * factor
        ag_buf[me] = summed.astype(jnp.bfloat16)

        @pl.loop(1, n)
        def _(k):
            ag_copy(k).start()

        view = ag_buf.at[pl.ds(0, pieces - 1)]
        pltpu.make_async_copy(view, view, ag_recv).wait()

    @pl.when(me >= pieces)
    def _():
        pltpu.make_async_copy(ag_buf, ag_buf, ag_recv).wait()

    sums_ref[...] = ag_buf[...]

    view = buf.at[pl.ds(0, chips - 1)]
    pltpu.make_async_copy(view, view, send_sem).wait()

    @pl.loop(0, pieces)
    def _(p):
        @pl.when(p != me)
        def _():
            piece_copy(p).wait_send()

    @pl.when(me < pieces)
    def _():
        pltpu.make_async_copy(ag_size, ag_size, ag_send).wait()


def unpack_kernel(fgrad_ref, sums_ref, fgrad_out, gw_in_ref, gb_in_ref, gw_out_ref):
    def unpack(first, count):
        rows = []
        for p in range(first, first + count):
            piece = sums_ref[p].astype(jnp.float32)
            rows.append(jnp.concatenate([piece[:8], piece[8:]], 1))
        return jnp.concatenate(rows, 0) if count > 1 else rows[0]

    in_pieces, out_pieces = gw_in_ref.shape[0] // 8, gw_out_ref.shape[0] // 8
    fgrad_out[...] = fgrad_ref[...]
    gw_in_ref[...] = unpack(0, in_pieces)
    gw_out_ref[...] = unpack(in_pieces, out_pieces)
    gb_in_ref[...] = unpack(in_pieces + out_pieces, 1)[:1]


def solution(mesh):
    R, C = mesh.shape["rows"], mesh.shape["cols"]
    n = R * C

    def body(inputs, task_ids, scale_table, probes, solves, alpha_solve, w_in, b_in, w_out):
        width, trials = inputs.shape
        hidden_width, feat_width = w_out.shape
        pieces = (width + feat_width) // 8 + 1
        operands = (
            inputs, task_ids[None, :], scale_table[None, :], probes, solves, alpha_solve[None, :], w_in, b_in[None, :],
            w_out.T,
        )
        staged = [pltpu.VMEM(a.shape, a.dtype) for a in operands]
        vmem = pl.BlockSpec(memory_space=pltpu.VMEM)
        fgrad, sums = pl.pallas_call(
            functools.partial(whole_kernel, R, C),
            out_shape=(
                jax.ShapeDtypeStruct((feat_width, trials), jnp.float32),
                jax.ShapeDtypeStruct((pieces, 16, LANES), jnp.bfloat16),
            ),
            in_specs=[pl.BlockSpec(memory_space=pltpu.HBM)] * 9,
            out_specs=(vmem,) * 2,
            scratch_shapes=staged
            + [
                pltpu.SemaphoreType.DMA((9,)),
                pltpu.VMEM((n // 2, trials // 2 + 16, LANES), jnp.bfloat16),
                pltpu.VMEM((2, 2, trials, LANES), jnp.bfloat16),
                pltpu.VMEM((2, trials, LANES), jnp.float32),
                pltpu.VMEM((pieces, 16, LANES), jnp.float32),
                pltpu.VMEM((n, 16, LANES), jnp.float32),
                pltpu.VMEM((pieces, 16, LANES), jnp.bfloat16),
                pltpu.VMEM((n - 1, 16, LANES), jnp.bfloat16),
                pltpu.SemaphoreType.DMA((n // 2,)),
                pltpu.SemaphoreType.DMA,
                pltpu.SemaphoreType.DMA((2,)),
                pltpu.SemaphoreType.DMA((2,)),
                pltpu.SemaphoreType.DMA((pieces,)),
                pltpu.SemaphoreType.DMA,
                pltpu.SemaphoreType.DMA,
                pltpu.SemaphoreType.DMA,
            ],
            compiler_params=pltpu.CompilerParams(
                collective_id=0, has_side_effects=True, vmem_limit_bytes=64 * 1024 * 1024
            ),
        )(*operands)
        fgrad, gw_in, gb_in, gw_out = pl.pallas_call(
            unpack_kernel,
            out_shape=(
                jax.ShapeDtypeStruct((feat_width, trials), jnp.float32),
                jax.ShapeDtypeStruct((width, hidden_width), jnp.float32),
                jax.ShapeDtypeStruct((1, hidden_width), jnp.float32),
                jax.ShapeDtypeStruct((feat_width, hidden_width), jnp.float32),
            ),
            in_specs=[vmem] * 2,
            out_specs=(vmem,) * 4,
            compiler_params=pltpu.CompilerParams(vmem_limit_bytes=64 * 1024 * 1024),
        )(fgrad, sums)
        return fgrad, gw_in, gb_in[0], jnp.transpose(gw_out)

    split = ("groups", "rows", "cols")
    return jax.shard_map(
        body,
        mesh=mesh,
        in_specs=(
            P(None, split), P(split), P(), P(None, split), P(None, split), P(split), P(), P(), P(),
        ),
        out_specs=(P(None, split), P("groups", None), P("groups"), P("groups", None)),
        check_vma=False,
    )
```

time: 32.6 us -> 28.5 us (0.87)
  local copies, waits for them, and re-layouts: 4.11 us -> 0 us
    unnamed x19 -> x0, local copies, waits for them, and re-layouts: 3.4 us -> none
    pallas_call x0 -> x1, Pallas kernels: none -> 1.51 us  [body(): pl.pallas_call(unpack_kernel, out_shape=(jax.ShapeDtypeStruct((feat_width...]
    pallas_call x1, Pallas kernels: 27.5 us -> 26.1 us  [body(): pl.pallas_call(functools.partial(whole_kernel, R, C), out_shape=(jax.Shap...]
    reshape x1 -> x0, local copies, waits for them, and re-layouts: 0.71 us -> none  [body(): table = jnp.pad(scale_table, (0, -tasks % (8 * LANES))).reshape(-1, LANES)]
where the time goes in v2:
time: 28.5 us; the launch traced here: 28.2 us
  Pallas kernels  27.6 us (97%)
  between operations  0.64 us (2%)
    pallas_call x1, Pallas kernels, body(): pl.pallas_call(functools.partial(whole_kernel, R, C), out_shape=(jax.Shap...  26.1 us
    pallas_call x1, Pallas kernels, body(): pl.pallas_call(unpack_kernel, out_shape=(jax.ShapeDtypeStruct((feat_width...  1.51 us

profile of v2, /device:TPU:0, one launch (start us, length us, event | category | flops | bytes accessed | tf_op | source)
XLA Modules:
  0.0 28.2 jit_solution(15840057923558185388)
XLA Ops:
  0.6 26.1 %shard_map.120 = (f32[64,192]{1,0:T(8,128)}, bf16[13,16,128]{2,1,0:T(8,128)(2,1)}) custom-call(bf16[32,192]{1,0:T(8,128)(2,1)} %refs_and_scratch_0_.1, s32[1,192]{1,0:T(1,128)} %bitcast.9, f32[1,3000]{1,0:T(1,128)} %bitcast.8, f32[16,192]{1,0:T(8,128)} %refs_and_scratch_3_.1, f32[16,192]{1,0:T(8,128)} %refs_and_scratch_4_.1, f32[1,192]{1,0:T(1,128)} %bitcast.10, ...), custom_call_target="tpu_custom_call" | custom-call | tf_op jit(solution)/shard_map/pallas_call | solution.py:373
  26.7 1.5 %shard_map.121 = (f32[64,192]{1,0:T(8,128)}, f32[32,256]{1,0:T(8,128)}, f32[1,256]{1,0:T(1,128)}, f32[64,256]{1,0:T(8,128)}) custom-call(f32[64,192]{1,0:T(8,128)} %get-tuple-element.10.fgrad_ref, bf16[13,16,128]{2,1,0:T(8,128)(2,1)} %get-tuple-element.11.sums_ref), custom_call_target="tpu_custom_call" | custom-call | tf_op jit(solution)/shard_map/pallas_call | solution.py:404

commit v3 on v2

--- a/solution.py
+++ b/solution.py
@@ -269,61 +269,75 @@
     total, weight_sum = mixed[:, :feat_width], mixed[:, feat_width : feat_width + 1]
     feat_grad = (total - weight_sum * feats_f) * (2.0 * rate)
     grad_feats = feat_grad.astype(jnp.bfloat16)
+    order = sorted(range(R), key=lambda k: abs(2 * k - R + 1))[:2]
+    owners = len(order) * C
+    rank = jnp.where(r == order[0], c, jnp.where(r == order[-1], (len(order) - 1) * C + c, owners))
+    held = -(-pieces // owners)
+
+    def owner(p):
+        q = lax.rem(p, owners)
+        return {"rows": jnp.where(q < C, order[0], order[-1]), "cols": lax.rem(q, C)}
+
+    def piece_copy(p):
+        return pltpu.make_async_remote_copy(
+            src_ref=parts.at[p], dst_ref=rs_buf.at[p // owners, me], send_sem=rs_send.at[p],
+            recv_sem=rs_recv.at[p // owners], device_id=owner(p), device_id_type=MESH,
+        )
+
+    def send_pieces(values, first):
+        count = values.shape[0] // 8
+        for p in range(count):
+            for h in range(2):
+                part = values[8 * p : 8 * p + 8, h * LANES : (h + 1) * LANES]
+                parts[first + p, 8 * h : 8 * h + 8] = part.astype(parts.dtype)
+
+        @pl.loop(first, first + count)
+        def _(p):
+            @pl.when(lax.rem(p, owners) != rank)
+            def _():
+                piece_copy(p).start()
+
+    g_out = lax.dot_general(
+        grad_feats, hidden, (((0,), (0,)), ((), ())), preferred_element_type=jnp.float32
+    )
+    send_pieces(g_out, 0)
     grad_hidden = jnp.dot(grad_feats, w_out_t, preferred_element_type=jnp.float32)
     grad_pre = grad_hidden * (sig * (1.0 + preact * (1.0 - sig)))
     g_in = jnp.dot(inputs, grad_pre.astype(jnp.bfloat16), preferred_element_type=jnp.float32)
-    g_out = lax.dot_general(
-        grad_feats, hidden, (((0,), (0,)), ((), ())), preferred_element_type=jnp.float32
-    )
     g_bias = jnp.broadcast_to(jnp.sum(grad_pre, 0, keepdims=True), (8, grad_pre.shape[1]))
-    packed = jnp.concatenate([g_in, g_out, g_bias], 0)
-    for p in range(pieces):
-        for h in range(2):
-            parts[p, 8 * h : 8 * h + 8] = packed[8 * p : 8 * p + 8, h * LANES : (h + 1) * LANES]
-
-    def piece_copy(p):
-        return pltpu.make_async_remote_copy(
-            src_ref=parts.at[p], dst_ref=rs_buf.at[me], send_sem=rs_send.at[p], recv_sem=rs_recv,
-            device_id=coords(p), device_id_type=MESH,
-        )
-
-    @pl.loop(0, pieces)
-    def _(k):
-        p = lax.rem(me + k, pieces)
-
-        @pl.when(p != me)
-        def _():
-            piece_copy(p).start()
+    send_pieces(jnp.concatenate([g_in, g_bias], 0), feat_width // 8)
 
     wide = jnp.concatenate([feat_grad, jnp.zeros((trials, LANES - feat_width), jnp.float32)], 1)
     wide = jnp.concatenate([wide, jnp.zeros((pad, LANES), jnp.float32)], 0)
     fgrad_ref[...] = jnp.transpose(wide)[:feat_width, :trials]
 
-    def ag_copy(k):
+    def ag_copy(p, k):
         return pltpu.make_async_remote_copy(
-            src_ref=ag_buf.at[me], dst_ref=ag_buf.at[me], send_sem=ag_send, recv_sem=ag_recv,
+            src_ref=ag_buf.at[p], dst_ref=ag_buf.at[p], send_sem=ag_send.at[p // owners], recv_sem=ag_recv.at[p],
             device_id=coords(other(k)), device_id_type=MESH,
         )
 
     factor = 1.0 / math.sqrt(trials * n)
-
-    @pl.when(me < pieces)
-    def _():
-        rs_buf[me] = parts[me]
-        pltpu.make_async_copy(rs_buf.at[pl.ds(0, n - 1)], rs_buf.at[pl.ds(0, n - 1)], rs_recv).wait()
-        summed = jnp.sum(rs_buf[...], 0) * factor
-        ag_buf[me] = summed.astype(jnp.bfloat16)
-
-        @pl.loop(1, n)
-        def _(k):
-            ag_copy(k).start()
-
-        view = ag_buf.at[pl.ds(0, pieces - 1)]
-        pltpu.make_async_copy(view, view, ag_recv).wait()
-
-    @pl.when(me >= pieces)
-    def _():
-        pltpu.make_async_copy(ag_buf, ag_buf, ag_recv).wait()
+    for h in range(held):
+        p = rank + h * owners
+
+        @pl.when((rank < owners) & (p < pieces))
+        def _():
+            rs_buf[h, me] = parts[p]
+            view = rs_buf.at[h, pl.ds(0, n - 1)]
+            pltpu.make_async_copy(view, view, rs_recv.at[h]).wait()
+            summed = jnp.sum(rs_buf[h].astype(jnp.float32), 0) * factor
+            ag_buf[p] = summed.astype(jnp.bfloat16)
+
+            @pl.loop(1, n)
+            def _(k):
+                ag_copy(p, k).start()
+
+    @pl.loop(0, pieces)
+    def _(p):
+        @pl.when(lax.rem(p, owners) != rank)
+        def _():
+            pltpu.make_async_copy(ag_buf.at[p], ag_buf.at[p], ag_recv.at[p]).wait()
 
     sums_ref[...] = ag_buf[...]
 
@@ -332,13 +346,14 @@
 
     @pl.loop(0, pieces)
     def _(p):
-        @pl.when(p != me)
+        @pl.when(lax.rem(p, owners) != rank)
         def _():
             piece_copy(p).wait_send()
 
-    @pl.when(me < pieces)
-    def _():
-        pltpu.make_async_copy(ag_size, ag_size, ag_send).wait()
+    for h in range(held):
+        @pl.when((rank < owners) & (rank + h * owners < pieces))
+        def _():
+            pltpu.make_async_copy(ag_size, ag_size, ag_send.at[h]).wait()
 
 
 def unpack_kernel(fgrad_ref, sums_ref, fgrad_out, gw_in_ref, gb_in_ref, gw_out_ref):
@@ -351,8 +366,8 @@
 
     in_pieces, out_pieces = gw_in_ref.shape[0] // 8, gw_out_ref.shape[0] // 8
     fgrad_out[...] = fgrad_ref[...]
-    gw_in_ref[...] = unpack(0, in_pieces)
-    gw_out_ref[...] = unpack(in_pieces, out_pieces)
+    gw_out_ref[...] = unpack(0, out_pieces)
+    gw_in_ref[...] = unpack(out_pieces, in_pieces)
     gb_in_ref[...] = unpack(in_pieces + out_pieces, 1)[:1]
 
 
@@ -369,6 +384,7 @@
             w_out.T,
         )
         staged = [pltpu.VMEM(a.shape, a.dtype) for a in operands]
+        held = -(-pieces // (min(R, 2) * C))
         vmem = pl.BlockSpec(memory_space=pltpu.VMEM)
         fgrad, sums = pl.pallas_call(
             functools.partial(whole_kernel, R, C),
@@ -384,8 +400,8 @@
                 pltpu.VMEM((n // 2, trials // 2 + 16, LANES), jnp.bfloat16),
                 pltpu.VMEM((2, 2, trials, LANES), jnp.bfloat16),
                 pltpu.VMEM((2, trials, LANES), jnp.float32),
-                pltpu.VMEM((pieces, 16, LANES), jnp.float32),
-                pltpu.VMEM((n, 16, LANES), jnp.float32),
+                pltpu.VMEM((pieces, 16, LANES), jnp.bfloat16),
+                pltpu.VMEM((held, n, 16, LANES), jnp.bfloat16),
                 pltpu.VMEM((pieces, 16, LANES), jnp.bfloat16),
                 pltpu.VMEM((n - 1, 16, LANES), jnp.bfloat16),
                 pltpu.SemaphoreType.DMA((n // 2,)),
@@ -393,14 +409,14 @@
                 pltpu.SemaphoreType.DMA((2,)),
                 pltpu.SemaphoreType.DMA((2,)),
                 pltpu.SemaphoreType.DMA((pieces,)),
-                pltpu.SemaphoreType.DMA,
-                pltpu.SemaphoreType.DMA,
-                pltpu.SemaphoreType.DMA,
+                pltpu.SemaphoreType.DMA((held,)),
+                pltpu.SemaphoreType.DMA((held,)),
+                pltpu.SemaphoreType.DMA((pieces,)),
             ],
             compiler_params=pltpu.CompilerParams(
-                collective_id=0, has_side_effects=True, vmem_limit_bytes=64 * 1024 * 1024
+                collective_id=0, has_side_effects=True, vmem_limit_bytes=48 * 1024 * 1024
             ),
-        )(*operands)
+        )(*[pltpu.with_memory_space_constraint(a, pltpu.HBM) for a in operands])
         fgrad, gw_in, gb_in, gw_out = pl.pallas_call(
             unpack_kernel,
             out_shape=(
@@ -411,7 +427,7 @@
             ),
             in_specs=[vmem] * 2,
             out_specs=(vmem,) * 4,
-            compiler_params=pltpu.CompilerParams(vmem_limit_bytes=64 * 1024 * 1024),
+            compiler_params=pltpu.CompilerParams(vmem_limit_bytes=4 * 1024 * 1024),
         )(fgrad, sums)
         return fgrad, gw_in, gb_in[0], jnp.transpose(gw_out)
 

time: 28.5 us -> 25.4 us (0.89)
  Pallas kernels: 27.6 us -> 24.6 us
    pallas_call x1, Pallas kernels: 26.1 us -> 23.9 us  [body(): pl.pallas_call(functools.partial(whole_kernel, R, C), out_shape=(jax.Shap...]
    pallas_call x1, Pallas kernels: 1.51 us -> 0.67 us  [body(): pl.pallas_call(unpack_kernel, out_shape=(jax.ShapeDtypeStruct((feat_width...]
where the time goes in v3:
time: 25.4 us; the launch traced here: 25.2 us
  Pallas kernels  24.6 us (97%)
  between operations  0.64 us (3%)
    pallas_call x1, Pallas kernels, body(): pl.pallas_call(functools.partial(whole_kernel, R, C), out_shape=(jax.Shap...  23.9 us
    pallas_call x1, Pallas kernels, body(): pl.pallas_call(unpack_kernel, out_shape=(jax.ShapeDtypeStruct((feat_width...  0.67 us

profile of v3, /device:TPU:0, one launch (start us, length us, event | category | flops | bytes accessed | tf_op | source)
XLA Modules:
  0.0 25.2 jit_solution(1238361444406091719)
XLA Ops:
  0.6 23.9 %shard_map.120 = (f32[64,192]{1,0:T(8,128)S(1)}, bf16[13,16,128]{2,1,0:T(8,128)(2,1)S(1)}) custom-call(bf16[32,192]{1,0:T(8,128)(2,1)} %refs_and_scratch_0_.1, s32[1,192]{1,0:T(1,128)} %bitcast.9, f32[1,3000]{1,0:T(1,128)} %bitcast.8, f32[16,192]{1,0:T(8,128)} %refs_and_scratch_3_.1, f32[16,192]{1,0:T(8,128)} %refs_and_scratch_4_.1, f32[1,192]{1,0:T(1,128)} %bitcast.10, ...), custom_call_target="tpu_custom_call" | custom-call | tf_op jit(solution)/shard_map/pallas_call | solution.py:389
  24.5 0.7 %shard_map.121 = (f32[64,192]{1,0:T(8,128)}, f32[32,256]{1,0:T(8,128)}, f32[1,256]{1,0:T(1,128)}, f32[64,256]{1,0:T(8,128)}) custom-call(f32[64,192]{1,0:T(8,128)S(1)} %get-tuple-element.10.fgrad_ref, bf16[13,16,128]{2,1,0:T(8,128)(2,1)S(1)} %get-tuple-element.11.sums_ref), custom_call_target="tpu_custom_call" | custom-call | tf_op jit(solution)/shard_map/pallas_call | solution.py:420

commit v4 on v3

--- a/solution.py
+++ b/solution.py
@@ -239,9 +239,7 @@
             )
         return jnp.concatenate(found, 0).astype(jnp.bfloat16)
 
-    def add_pair(p, carry):
-        total, sums = carry
-        cols = columns((here // 2) ^ p)
+    def add_columns(cols, total, sums):
         both = lax.dot_general(left, cols, (((1,), (1,)), ((), ())), preferred_element_type=jnp.float32)
         weight = both[2 * trials :] * jnp.exp(both[: 2 * trials])
         for j in range(2 * trials // LANES):
@@ -250,22 +248,28 @@
         return total, sums
 
     def step(p, carry):
+        cols, total, sums = carry
         wait_chip(2 * p)
         wait_chip(2 * p + 1)
-        return add_pair(p, carry)
+        later = columns((here // 2) ^ p)
+        return (later, *add_columns(cols, total, sums))
 
     empty = jnp.zeros((2 * trials, LANES), jnp.float32)
     wait_chip(1)
-    carry = add_pair(0, (empty, empty))
-    total, sums = lax.fori_loop(1, chips // 2, step, carry)
-
-    weight_sum = jnp.sum(sums, 1, keepdims=True)
-    lane4 = lax.broadcasted_iota(jnp.int32, (2 * trials, LANES), 1)
-    mixed = jnp.where(lane4 < feat_width, total, weight_sum)
-    swap[0] = mixed[trials:]
+    carry = (columns(here // 2), empty, empty)
+    for p in range(1, chips // 2):
+        carry = step(p, carry)
+    total, sums = add_columns(*carry)
+
+    def share(first):
+        weight_sum = jnp.sum(sums[first : first + trials], 1, keepdims=True)
+        return jnp.where(lane2 < feat_width, total[first : first + trials], weight_sum)
+
+    swap[0] = share(trials)
     core_copy(swap, 1).start()
+    mixed = share(0)
     core_copy(swap, 1).wait()
-    mixed = mixed[:trials] + swap[1]
+    mixed = mixed + swap[1]
     total, weight_sum = mixed[:, :feat_width], mixed[:, feat_width : feat_width + 1]
     feat_grad = (total - weight_sum * feats_f) * (2.0 * rate)
     grad_feats = feat_grad.astype(jnp.bfloat16)
@@ -304,7 +308,8 @@
     grad_hidden = jnp.dot(grad_feats, w_out_t, preferred_element_type=jnp.float32)
     grad_pre = grad_hidden * (sig * (1.0 + preact * (1.0 - sig)))
     g_in = jnp.dot(inputs, grad_pre.astype(jnp.bfloat16), preferred_element_type=jnp.float32)
-    g_bias = jnp.broadcast_to(jnp.sum(grad_pre, 0, keepdims=True), (8, grad_pre.shape[1]))
+    bias_terms = split3(jnp.sum(grad_pre, 0, keepdims=True))
+    g_bias = jnp.concatenate([*bias_terms, jnp.zeros((5, hidden_width), jnp.float32)], 0)
     send_pieces(jnp.concatenate([g_in, g_bias], 0), feat_width // 8)
 
     wide = jnp.concatenate([feat_grad, jnp.zeros((trials, LANES - feat_width), jnp.float32)], 1)
@@ -368,7 +373,7 @@
     fgrad_out[...] = fgrad_ref[...]
     gw_out_ref[...] = unpack(0, out_pieces)
     gw_in_ref[...] = unpack(out_pieces, in_pieces)
-    gb_in_ref[...] = unpack(in_pieces + out_pieces, 1)[:1]
+    gb_in_ref[...] = jnp.sum(unpack(in_pieces + out_pieces, 1), 0, keepdims=True)
 
 
 def solution(mesh):

time: 25.4 us -> 24.9 us (0.980)
  Pallas kernels: 24.6 us -> 24 us
    pallas_call x1, Pallas kernels: 23.9 us -> 23.4 us  [body(): pl.pallas_call(functools.partial(whole_kernel, R, C), out_shape=(jax.Shap...]
where the time goes in v4:
time: 24.9 us; the launch traced here: 24.7 us
  Pallas kernels  24 us (96%)
  between operations  0.64 us (3%)
    pallas_call x1, Pallas kernels, body(): pl.pallas_call(functools.partial(whole_kernel, R, C), out_shape=(jax.Shap...  23.4 us
    pallas_call x1, Pallas kernels, body(): pl.pallas_call(unpack_kernel, out_shape=(jax.ShapeDtypeStruct((feat_width...  0.67 us

profile of v4, /device:TPU:0, one launch (start us, length us, event | category | flops | bytes accessed | tf_op | source)
XLA Modules:
  0.0 24.7 jit_solution(11332245483148883922)
XLA Ops:
  0.6 23.4 %shard_map.120 = (f32[64,192]{1,0:T(8,128)S(1)}, bf16[13,16,128]{2,1,0:T(8,128)(2,1)S(1)}) custom-call(bf16[32,192]{1,0:T(8,128)(2,1)} %refs_and_scratch_0_.1, s32[1,192]{1,0:T(1,128)} %bitcast.9, f32[1,3000]{1,0:T(1,128)} %bitcast.8, f32[16,192]{1,0:T(8,128)} %refs_and_scratch_3_.1, f32[16,192]{1,0:T(8,128)} %refs_and_scratch_4_.1, f32[1,192]{1,0:T(1,128)} %bitcast.10, ...), custom_call_target="tpu_custom_call" | custom-call | tf_op jit(solution)/shard_map/pallas_call | solution.py:394
  24.0 0.7 %shard_map.121 = (f32[64,192]{1,0:T(8,128)}, f32[32,256]{1,0:T(8,128)}, f32[1,256]{1,0:T(1,128)}, f32[64,256]{1,0:T(8,128)}) custom-call(f32[64,192]{1,0:T(8,128)S(1)} %get-tuple-element.10.fgrad_ref, bf16[13,16,128]{2,1,0:T(8,128)(2,1)S(1)} %get-tuple-element.11.sums_ref), custom_call_target="tpu_custom_call" | custom-call | tf_op jit(solution)/shard_map/pallas_call | solution.py:425

commit v5 on v4

--- a/solution.py
+++ b/solution.py
@@ -45,7 +45,7 @@
         return {"rows": q // C, "cols": lax.rem(q, C)}
 
     def other(k):
-        return lax.rem(me + k, n)
+        return me ^ (n - k)
 
     barrier = pltpu.get_barrier_semaphore()
 
@@ -257,8 +257,7 @@
     empty = jnp.zeros((2 * trials, LANES), jnp.float32)
     wait_chip(1)
     carry = (columns(here // 2), empty, empty)
-    for p in range(1, chips // 2):
-        carry = step(p, carry)
+    carry = lax.fori_loop(1, chips // 2, step, carry, unroll=chips <= 8)
     total, sums = add_columns(*carry)
 
     def share(first):

time: 24.9 us -> 25 us (level)
  no operation moved by 1% of the time
where the time goes in v5:
time: 25 us; the launch traced here: 24.8 us
  Pallas kernels  24.2 us (97%)
  between operations  0.64 us (3%)
    pallas_call x1, Pallas kernels, body(): pl.pallas_call(functools.partial(whole_kernel, R, C), out_shape=(jax.Shap...  23.5 us
    pallas_call x1, Pallas kernels, body(): pl.pallas_call(unpack_kernel, out_shape=(jax.ShapeDtypeStruct((feat_width...  0.67 us

profile of v5, /device:TPU:0, one launch (start us, length us, event | category | flops | bytes accessed | tf_op | source)
XLA Modules:
  0.0 24.8 jit_solution(13310797958368400665)
XLA Ops:
  0.6 23.5 %shard_map.120 = (f32[64,192]{1,0:T(8,128)S(1)}, bf16[13,16,128]{2,1,0:T(8,128)(2,1)S(1)}) custom-call(bf16[32,192]{1,0:T(8,128)(2,1)} %refs_and_scratch_0_.1, s32[1,192]{1,0:T(1,128)} %bitcast.9, f32[1,3000]{1,0:T(1,128)} %bitcast.8, f32[16,192]{1,0:T(8,128)} %refs_and_scratch_3_.1, f32[16,192]{1,0:T(8,128)} %refs_and_scratch_4_.1, f32[1,192]{1,0:T(1,128)} %bitcast.10, ...), custom_call_target="tpu_custom_call" | custom-call | tf_op jit(solution)/shard_map/pallas_call | solution.py:393
  24.1 0.7 %shard_map.121 = (f32[64,192]{1,0:T(8,128)}, f32[32,256]{1,0:T(8,128)}, f32[1,256]{1,0:T(1,128)}, f32[64,256]{1,0:T(8,128)}) custom-call(f32[64,192]{1,0:T(8,128)S(1)} %get-tuple-element.10.fgrad_ref, bf16[13,16,128]{2,1,0:T(8,128)(2,1)S(1)} %get-tuple-element.11.sums_ref), custom_call_target="tpu_custom_call" | custom-call | tf_op jit(solution)/shard_map/pallas_call | solution.py:424
